TPU v7x, 256 devices: a whole 4x4x8 slice. The times are simulated.
256 devices in a mesh: gr: 32 (over z_hi, y, core), gc: 8 (over x, z_lo).
Axes of the slice: x: 4, y: 4, z: 8 (z_hi: 4, z_lo: 2; z = z_hi * 2 + z_lo), core: 2. Of those that a mesh axis runs over, the one named last changes fastest.
Arguments:
- counts: int32 [40960, 16384], P('gr', 'gc'), may hold values from 0 to 1600
- row_ids: int32 [40960], P('gr'), may hold values from 0 to 40959, each once
- col_ids: int32 [16384], P('gc'), may hold values from 0 to 16383, each once
- row_marginal: int32 [40960], replicated, may hold values from 50000 to 999999
- col_marginal: int32 [16384], replicated, may hold values from 50000 to 999999
- row_emb: float32 [40960, 256], P(('gr', 'gc')), may hold values from -1.5 to 1.5
- row_acc: float32 [40960, 256], P(('gr', 'gc')), may hold values from 0.5 to 20
- col_emb: float32 [16384, 256], P(('gc', 'gr')), may hold values from -1.5 to 1.5
- col_acc: float32 [16384, 256], P(('gc', 'gr')), may hold values from 0.5 to 20
Outputs:
- row_new: float32 [40960, 256], P(('gr', 'gc'))
- row_acc_new: float32 [40960, 256], P(('gr', 'gc'))
- col_new: float32 [16384, 256], P(('gc', 'gr'))
- col_acc_new: float32 [16384, 256], P(('gc', 'gr'))
Inputs may be any that keep to these rules, and one draw needn't show every extreme that they name: `row_ids`: a permutation of the row ids. `col_ids`: a permutation of the column ids.
All inputs are finite; a program needn't handle non-finite values.
Results may differ from a plain program's by a relative error of at most 0.0082.
Values may be sent and summed in bfloat16 or wider, within the bound.
A program may use at most 64 MiB of HBM per device.

v0:
```python
import math

import jax
import jax.numpy as jnp
from jax import lax
from jax.sharding import PartitionSpec as P

learn_rate = 0.5


def block_grad(cnt, row_log, col_log, log_total, rows_half, cols_half, factor):
    score = lax.dot_general(
        rows_half, cols_half, (((1,), (1,)), ((), ())), preferred_element_type=jnp.float32
    )
    pmi = (
        jnp.log(jnp.maximum(cnt, 1).astype(jnp.float32))
        + log_total
        - row_log[:, None]
        - col_log[None, :]
    )
    diff = score - pmi
    confid = 0.1 + 0.25 * jnp.sqrt(cnt.astype(jnp.float32))
    grad = jnp.where(cnt > 0, confid * diff, jax.nn.sigmoid(diff)) * factor
    grad_half = grad.astype(jnp.bfloat16)
    row_part = jnp.dot(grad_half, cols_half, preferred_element_type=jnp.float32)
    col_part = lax.dot_general(
        grad_half, rows_half, (((0,), (0,)), ((), ())), preferred_element_type=jnp.float32
    )
    return (row_part, col_part)


def adagrad(emb, acc, grad):
    acc_new = acc + grad * grad
    return (emb - learn_rate * grad / jnp.sqrt(acc_new), acc_new)


def local(counts, row_ids, col_ids, row_marginal, col_marginal, row_emb, row_acc, col_emb, col_acc):
    shard_rows, shard_cols = counts.shape
    log_total = jnp.log(jnp.sum(row_marginal.astype(jnp.float32)))
    row_log = jnp.log(jnp.take(row_marginal, row_ids).astype(jnp.float32))
    col_log = jnp.log(jnp.take(col_marginal, col_ids).astype(jnp.float32))
    factor = 1.0 / math.sqrt(shard_cols * lax.axis_size("gc"))
    row_half = row_emb.astype(jnp.bfloat16)
    col_half = col_emb.astype(jnp.bfloat16)
    cols_whole = lax.all_gather(col_half, "gr", axis=0, tiled=True)
    row_part, col_part = block_grad(
        counts,
        row_log,
        col_log,
        log_total,
        lax.all_gather(row_half, "gc", axis=0, tiled=True),
        cols_whole,
        factor,
    )
    row_total = lax.psum(row_part, "gc")
    col_total = lax.psum(col_part, "gr")
    own_rows = lax.dynamic_slice_in_dim(
        row_total, lax.axis_index("gc") * row_emb.shape[0], row_emb.shape[0], 0
    )
    own_cols = lax.dynamic_slice_in_dim(
        col_total, lax.axis_index("gr") * col_emb.shape[0], col_emb.shape[0], 0
    )
    row_new, row_acc_new = adagrad(row_emb, row_acc, own_rows)
    col_new, col_acc_new = adagrad(col_emb, col_acc, own_cols)
    return (row_new, row_acc_new, col_new, col_acc_new)


def solution(mesh):
    placed = (
        P("gr", "gc"),
        P("gr"),
        P("gc"),
        P(),
        P(),
        P(("gr", "gc"), None),
        P(("gr", "gc"), None),
        P(("gc", "gr"), None),
        P(("gc", "gr"), None),
    )
    return jax.shard_map(
        local,
        mesh=mesh,
        in_specs=placed,
        out_specs=(
            P(("gr", "gc"), None),
            P(("gr", "gc"), None),
            P(("gc", "gr"), None),
            P(("gc", "gr"), None),
        ),
        check_vma=False,
    )
```

profile of v0, /device:TPU:1, one launch (start us, length us, event | category | flops | bytes accessed | tf_op | source)
XLA Modules:
  0.0 476.1 jit_solution(11806293137024662234)
XLA Ops:
  7.2 0.0 copy-start
  7.2 0.0 all-gather.2.cloned.1.call-start
  7.2 1.5 convert_element_type.30
  8.7 0.0 all-gather.2.cloned.1.call-update
  8.7 0.0 all-reduce.3.cloned.1.call-start
  8.8 0.9 convert_element_type.29
  9.7 0.7 compare_select_fusion.1
  10.4 6.8 %gather_fusion = s32[1280]{0:T(1024)S(1)} fusion(s32[40960]{0:T(1024)} %param.12, s32[2048]{0:T(1024)S(1)} %pad_clamp_fusion), kind=kCustom, calls=%fused_computation | custom fusion | bytes 15360 | tf_op jit(solution)/shard_map/jit(_take)/gather | solution.py:40
  17.2 1.6 convert_reduce_fusion
  19.5 0.7 fusion
  20.2 11.8 %gather_fusion.1 = s32[2048]{0:T(1024)S(1)} fusion(s32[16384]{0:T(1024)S(1)} %copy-done, s32[2048]{0:T(1024)S(1)} %fusion), kind=kCustom, calls=%fused_computation.1 | custom fusion | bytes 24576 | tf_op jit(solution)/shard_map/jit(_take)/gather | solution.py:41
  32.0 27.4 %all_gather.6 = bf16[1280,256]{1,0:T(8,128)(2,1)S(1)} all-gather(bf16[160,256]{1,0:T(8,128)(2,1)S(1)} %convert_element_type.29), channel_id=1, replica_groups=mesh['gr'=32,'gc'=8] {'gc'}, dimensions={0}, use_global_device_ids=true | all-gather | bytes 737280 | tf_op jit(solution)/shard_map/all_gather | solution.py:51
  59.5 8.7 %all-gather.2.cloned.1.call-done = bf16[2048,256]{1,0:T(8,128)(2,1)} async-done(((bf16[64,256]{1,0:T(8,128)(2,1)}), bf16[2048,256]{1,0:T(8,128)(2,1)}) %all-gather.2.cloned.1.call-update) | async-done | bytes 1048592 | tf_op jit(solution)/shard_map/all_gather | solution.py:45
  68.1 15.5 %multiply_convert_fusion = bf16[1280,2048]{1,0:T(8,128)(2,1)S(1)} fusion(s32[1280,2048]{1,0:T(8,128)} %param.9, bf16[1280,256]{1,0:T(8,128)(2,1)S(1)} %all_gather.6, bf16[2048,256]{1,0:T(8,128)(2,1)} %all-gather.2.cloned.1.call-done, f32[2048]{0:T(1024)S(1)} %convert_log_fusion, f32[1280]{0:T(1024)S(1)} %convert_log_fusion.1, f32[]{:T(128)S(6)} %log.17), kind=kOutput, calls=%fused_computation.2 | convolution fusion | flops 1386741760 | bytes 17445892 | tf_op jit(solution)/shard_map/dot_general | solution.py:12
  83.6 2.3 copy-done.8
  85.9 2.7 fusion.1
  88.6 0.0 all-reduce.3.cloned.1.call-update
  88.6 0.0 all-reduce.5.cloned.1.call-start
  88.7 5.5 %fusion.2 = f32[2048,256]{1,0:T(8,128)} fusion(bf16[1280,2048]{1,0:T(8,128)(2,1)} %copy-done.8, bf16[1280,256]{1,0:T(8,128)(2,1)S(1)} %all_gather.6), kind=kOutput, calls=%fused_computation.15 | convolution fusion | flops 1342177280 | bytes 7995392 | tf_op jit(solution)/shard_map/dot_general | solution.py:26
  94.2 0.0 all-reduce.5.cloned.1.call-update
  94.2 76.9 %all-reduce.3.cloned.1.call-done = f32[1280,256]{1,0:T(8,128)} async-done(((f32[1280,256]{1,0:T(8,128)}), f32[1280,256]{1,0:T(8,128)}) %all-reduce.3.cloned.1.call-update) | async-done | bytes 1310736 | tf_op jit(solution)/shard_map/psum | solution.py:55
  171.2 1.7 multiply_subtract_fusion
  172.8 295.2 %all-reduce.5.cloned.1.call-done = f32[2048,256]{1,0:T(8,128)} async-done(((f32[2048,256]{1,0:T(8,128)}), f32[2048,256]{1,0:T(8,128)}) %all-reduce.5.cloned.1.call-update) | async-done | bytes 2097168 | tf_op jit(solution)/shard_map/psum | solution.py:56
  468.1 1.5 multiply_subtract_fusion.1
  (19 shorter events, 0.1 us)
Async XLA Ops:
  7.2 13.0 %copy-start = (s32[16384]{0:T(1024)S(1)}, s32[16384]{0:T(1024)}, u32[]{:S(2)}) copy-start(s32[16384]{0:T(1024)} %param.13) | copy-start | bytes 196612
  7.2 24.8 %copy-start.6 = (s32[1280]{0:T(1024)S(1)}, s32[1280]{0:T(1024)}, u32[]{:S(2)}) copy-start(s32[1280]{0:T(1024)} %param.10) | copy-start | bytes 15364
  7.2 24.8 %copy-start.5 = (s32[2048]{0:T(1024)S(1)}, s32[2048]{0:T(1024)}, u32[]{:S(2)}) copy-start(s32[2048]{0:T(1024)} %param.11) | copy-start | bytes 24580
  7.2 60.9 %all-gather.2.cloned.1.call-start = ((), (), s32[]{:S(2)}) async-start(), calls=%async_computation | async-start | bytes 1081344 | tf_op jit(solution)/shard_map/all_gather | solution.py:45
  8.7 162.4 %all-reduce.3.cloned.1.call-start = ((), (), s32[]{:S(2)}) async-start(), calls=%async_computation.1 | async-start | bytes 2621440 | tf_op jit(solution)/shard_map/psum | solution.py:55
  68.1 17.8 %copy-start.7 = (bf16[2048,256]{1,0:T(8,128)(2,1)S(1)}, bf16[2048,256]{1,0:T(8,128)(2,1)}, u32[]{:S(2)}) copy-start(bf16[2048,256]{1,0:T(8,128)(2,1)} %all-gather.2.cloned.1.call-done) | copy-start | bytes 3145732
  83.6 2.3 copy-start.8
  88.6 82.6 %copy-start.1 = (f32[160,256]{1,0:T(8,128)S(1)}, f32[160,256]{1,0:T(8,128)}, u32[]{:S(2)}) copy-start(f32[160,256]{1,0:T(8,128)} %param.14) | copy-start | bytes 491524
  88.6 82.6 %copy-start.3 = (f32[160,256]{1,0:T(8,128)S(1)}, f32[160,256]{1,0:T(8,128)}, u32[]{:S(2)}) copy-start(f32[160,256]{1,0:T(8,128)} %param.15) | copy-start | bytes 491524
  88.6 379.5 %copy-start.2 = (f32[64,256]{1,0:T(8,128)S(1)}, f32[64,256]{1,0:T(8,128)}, u32[]{:S(2)}) copy-start(f32[64,256]{1,0:T(8,128)} %param.16) | copy-start | bytes 196612
  88.6 379.5 %copy-start.4 = (f32[64,256]{1,0:T(8,128)S(1)}, f32[64,256]{1,0:T(8,128)}, u32[]{:S(2)}) copy-start(f32[64,256]{1,0:T(8,128)} %param.17) | copy-start | bytes 196612
  88.6 379.4 %all-reduce.5.cloned.1.call-start = ((), (), s32[]{:S(2)}) async-start(), calls=%async_computation.2 | async-start | bytes 4194304 | tf_op jit(solution)/shard_map/psum | solution.py:56
Sparse Core Ops, SparseCore 0:
  11.2 56.9 all-gather.1
  88.7 82.3 all-reduce.2
  173.8 294.2 all-reduce.4
where the time goes:
time: 476 us
  waiting for transfers between devices  381 us (80%)
  blocking collectives  27.4 us (6%)
  matrix products  23.7 us (5%)
  local copies, waits for them, and re-layouts  20.9 us (4%)
  between operations  14.5 us (3%)
  other arithmetic  8.56 us (2%)
    psum x1, waiting for transfers between devices, local(): col_total = lax.psum(col_part, 'gr')  295 us
    psum x1, waiting for transfers between devices, local(): row_total = lax.psum(row_part, 'gc')  76.9 us
    all_gather x1, blocking collectives, local(): lax.all_gather(row_half, 'gc', axis=0, tiled=True)  27.4 us
    dot_general x1, matrix products, block_grad(): lax.dot_general(rows_half, cols_half, (((1,), (1,)), ((), ())), preferred...  15.5 us
    gather x1, local copies, waits for them, and re-layouts, local(): col_log = jnp.log(jnp.take(col_marginal, col_ids).astype(jnp.float32))  11.8 us
  transfers between devices with their start and end apart: 3, of which 3 were waited for; matrix products, arithmetic and copies ran while one was open for 6% of the time, Pallas kernels for 0%

commit v1 on v0

v1 whole, which is shorter than its diff:
```python
import functools

import jax
import jax.numpy as jnp
from jax import lax
from jax.experimental import pallas as pl
from jax.experimental.pallas import tpu as pltpu
from jax.sharding import PartitionSpec as P

F32 = jnp.float32
BF16 = jnp.bfloat16
MESH = pl.DeviceIdType.MESH

LEARN_RATE = 0.5
K = 256
NX, NZL = 4, 2
NZH, NY, NC = 4, 4, 2
RB = 160
CB = 64
XB = RB * NZL
QB = NZH * NC * CB
ROWS = NX * XB
COLS = NY * QB
SUB = 16
Q_STEPS = (1, 2, 3, 0)
X_FIRST = (0, 1, 3, 2)
X_LAST = (2, 1, 3, 0)
N_SEMS = 64


def lookup(table, ids):
    high = lax.shift_right_logical(ids, 7)
    low = ids & 127
    n_high, n = table.shape[0], ids.shape[1]
    hot = (lax.broadcasted_iota(jnp.int32, (n_high, n), 0) == high).astype(F32).astype(BF16)
    digits = [
        lax.shift_right_logical(table, 16),
        lax.shift_right_logical(table, 8) & 255,
        table & 255,
    ]
    parts = [
        jnp.dot(d.astype(F32).T.astype(BF16), hot, preferred_element_type=F32) for d in digits
    ]
    whole = parts[0] * 65536.0 + parts[1] * 256.0 + parts[2]
    mine = lax.broadcasted_iota(jnp.int32, (128, n), 0) == low
    return jnp.log(jnp.sum(jnp.where(mine, whole, 0.0), axis=0, keepdims=True))


def kernel(
    cnt_hbm, rid_hbm, cid_hbm, rmar_hbm, cmar_hbm, remb_hbm, racc_hbm, cemb_hbm, cacc_hbm,
    rnew_ref, raccn_ref, cnew_ref, caccn_ref,
    cnt, rid, cid, rmar, cmar, remb, racc, cemb, cacc,
    rows, rows_t, cols, cols_t, row_term, col_term,
    s_ref, g_ref, row_part, col_tmp, col_part, q_sum,
    ex_s, ex_r, y2p_s, y2p_r, y2m_s, y2m_r, y3p_s, y3p_r, y3m_s, y3m_r,
    z2p_s, z2p_r, z2m_s, z2m_r, z3p_s, z3p_r, z3m_s, z3m_r,
    x2p_s, x2p_r, x2m_s, x2m_r, x3p_s, x3p_r, x3m_s, x3m_r, w_s, w_r,
    local_sem, send_sem, recv_sem,
):
    gr = lax.axis_index("gr")
    gc = lax.axis_index("gc")
    c = lax.rem(gr, NC)
    y = lax.rem(gr // NC, NY)
    zh = gr // (NC * NY)
    zl = lax.rem(gc, NZL)
    x = gc // NZL

    def at(dx=0, dzl=0, dzh=0, dy=0, dc=0):
        g = (lax.rem(zh + dzh, NZH) * NY + lax.rem(y + dy, NY)) * NC + lax.rem(c + dc, NC)
        k = lax.rem(x + dx, NX) * NZL + lax.rem(zl + dzl, NZL)
        return (g, k)

    ZP, ZM = at(dzh=1), at(dzh=3)
    YP, YM = at(dy=1), at(dy=3)
    XP, XM = at(dx=1), at(dx=3)
    CO, LO = at(dc=1), at(dzl=1)
    neighbours = (ZP, ZM, YP, YM, XP, XM, CO, LO)

    loads = []

    def load(src, dst):
        cp = pltpu.make_async_copy(src, dst, local_sem.at[len(loads)])
        cp.start()
        loads.append(cp)
        return cp

    l_remb, l_cemb = load(remb_hbm, remb), load(cemb_hbm, cemb)
    barrier = pltpu.get_barrier_semaphore()
    for n in neighbours:
        pl.semaphore_signal(barrier, inc=1, device_id=n, device_id_type=MESH)
    l_ids = [load(rid_hbm, rid), load(cid_hbm, cid), load(rmar_hbm, rmar), load(cmar_hbm, cmar)]
    l_cnt = [
        load(cnt_hbm.at[pl.ds(i * XB, XB)], cnt.at[pl.ds(i * XB, XB)]) for i in range(NX)
    ]
    l_acc = [load(racc_hbm, racc), load(cacc_hbm, cacc)]

    copies = []

    def send(src, dst, target):
        i = len(copies)
        cp = pltpu.make_async_remote_copy(
            src_ref=src, dst_ref=dst, send_sem=send_sem.at[i], recv_sem=recv_sem.at[i],
            device_id=target, device_id_type=MESH,
        )
        cp.start()
        copies.append(cp)
        return cp

    def zz(d):
        return lax.rem(zh + d, NZH)

    def yy(d):
        return lax.rem(y + d, NY)

    def xx(d):
        return lax.rem(x + d, NX)

    def same(ref, target):
        return send(ref, ref, target)

    l_remb.wait()
    rows[x, zl] = (remb[...] * 0.5).astype(BF16)
    l_cemb.wait()
    cols[y, zh, c] = cemb[...].astype(BF16)
    pl.semaphore_wait(barrier, len(neighbours))

    own_r, own_c = rows.at[x, zl], cols.at[y, zh, c]
    r_lo = same(own_r, LO)
    r_p0, r_m0 = same(own_r, XP), same(own_r, XM)
    c_zp, c_zm = same(own_c, ZP), same(own_c, ZM)
    c_yp, c_ym = {0: same(own_c, YP)}, {0: same(own_c, YM)}

    for cp in l_ids:
        cp.wait()
    col_log = lookup(cmar[...], cid[...])
    col_term[...] = jnp.broadcast_to(0.5 * col_log, col_term.shape)
    r_lo.wait_recv()
    other_r = rows.at[x, 1 - zl]
    r_p1, r_m1 = same(other_r, XP), same(other_r, XM)
    c_zp.wait_recv()
    c_zfp = same(cols.at[y, zz(3), c, pl.ds(0, 32)], ZP)
    c_yp[3], c_ym[3] = same(cols.at[y, zz(3), c], YP), same(cols.at[y, zz(3), c], YM)
    c_zm.wait_recv()
    c_zfm = same(cols.at[y, zz(1), c, pl.ds(32, 32)], ZM)
    c_yp[1], c_ym[1] = same(cols.at[y, zz(1), c], YP), same(cols.at[y, zz(1), c], YM)
    c_yp[0].wait_recv()
    c_yfp = {0: same(cols.at[yy(3), zh, c], YP)}
    row_log = lookup(rmar[...], rid[...])
    log_total = jnp.log(jnp.sum(rmar[...].astype(F32)))
    row_vec = 0.5 * (row_log - log_total)
    for b in range(ROWS // 128):
        piece = jnp.broadcast_to(row_vec[:, b * 128 : (b + 1) * 128], (128, 128))
        row_term[b * 128 : (b + 1) * 128, :] = piece.T
    c_zfp.wait_recv()
    c_zfm.wait_recv()
    c_yp[2], c_ym[2] = same(cols.at[y, zz(2), c], YP), same(cols.at[y, zz(2), c], YM)
    core = {0: same(cols.at[y, :, c], CO)}
    r_p0.wait_recv()
    r_fp = same(rows.at[xx(3), zl], XP)
    c_ym[3].wait_recv()
    c_yfm = {3: same(cols.at[yy(1), zz(3), c], YM)}
    c_ym[1].wait_recv()
    c_yfm[1] = same(cols.at[yy(1), zz(1), c], YM)
    r_m1.wait_recv()
    r_fm = same(rows.at[xx(1), 1 - zl], XM)
    c_yp[2].wait_recv()
    c_yfp[2] = same(cols.at[yy(3), zz(2), c], YP)
    c_ym[0].wait_recv()
    c_ym[2].wait_recv()
    core[1] = same(cols.at[yy(1), :, c], CO)
    c_yp[1].wait_recv()
    c_yp[3].wait_recv()
    core[3] = same(cols.at[yy(3), :, c], CO)
    r_m0.wait_recv()
    r_p1.wait_recv()
    for cp in (c_yfp[0], c_yfm[3], c_yfm[1], c_yfp[2]):
        cp.wait_recv()
    core[2] = same(cols.at[yy(2), :, c], CO)
    r_fp.wait_recv()
    r_fm.wait_recv()
    for i in range(NX):
        rows_t[:, i * XB : (i + 1) * XB] = rows[i].reshape(XB, K).T
    for d in Q_STEPS:
        core[d].wait_recv()
        cols_t[yy(d)] = cols[yy(d)].reshape(QB, K).T
    for cp in l_cnt:
        cp.wait()

    def score(s, i):
        q, dx = yy(Q_STEPS[s]), x_order(s)[i]
        s_ref[i % 2] = jnp.dot(
            rows[xx(dx)].reshape(XB, K), cols_t[q], preferred_element_type=F32
        )

    def x_order(s):
        return X_LAST if s == NY - 1 else X_FIRST

    def elem(s, i):
        q, r_at = yy(Q_STEPS[s]), pl.multiple_of(xx(x_order(s)[i]) * XB, XB)
        for z in range(NZH):
            c_at = pl.multiple_of(z * QB + q * 128, 128)
            c_row = col_term[:, pl.ds(c_at, 128)]
            for u in range(XB // SUB):
                at_u = pl.ds(pl.multiple_of(r_at + u * SUB, SUB), SUB)
                n = cnt[at_u, pl.ds(c_at, 128)]
                m = jnp.maximum(n, 1).astype(F32)
                inv = lax.rsqrt(m)
                half = (
                    s_ref[i % 2, u * SUB : (u + 1) * SUB, z * 128 : (z + 1) * 128] + jnp.log(inv)
                ) + (row_term[at_u, :] + c_row)
                g = jnp.where(n > 0, (m * inv + 0.4) * half, jnp.tanh(half) + 1.0)
                g_ref[s % 2, at_u, z * 128 : (z + 1) * 128] = g.astype(BF16)

    def row_grad(s, i):
        q, at_x = yy(Q_STEPS[s]), xx(x_order(s)[i])
        r_at = pl.multiple_of(at_x * XB, XB)
        part = jnp.dot(
            g_ref[s % 2, pl.ds(r_at, XB), :], cols[q].reshape(QB, K), preferred_element_type=F32
        ).reshape(NZL, RB, K)
        if s == 0:
            row_part[at_x] = part
        else:
            row_part[at_x] += part

    def col_grad(s):
        t = jnp.dot(rows_t[...], g_ref[s % 2], preferred_element_type=F32)
        col_tmp[s % 2] = t.T.reshape(NZH, NC, CB, K)
        ex_s[s] = col_tmp[s % 2, :, 1 - c].astype(BF16)
        col_part[s] = col_tmp[s % 2, :, c]
        return send(ex_s.at[s], ex_r.at[s], CO)

    ex, hop = {}, {}

    def y_far():
        ex[1].wait_recv()
        total = col_part[1] + ex_r[1].astype(F32)
        y2p_s[...] = total[0:2].astype(BF16)
        y2m_s[...] = total[2:4].astype(BF16)
        hop["y2p"] = send(y2p_s, y2p_r, YP)
        hop["y2m"] = send(y2m_s, y2m_r, YM)

    def y_up():
        ex[0].wait_recv()
        hop["y2p"].wait_recv()
        total = col_part[0] + ex_r[0].astype(F32)
        y3p_s[0:2] = (total[0:2] + y2p_r[...].astype(F32)).astype(BF16)
        y3p_s[2:4] = total[2:4].astype(BF16)
        hop["y3p"] = send(y3p_s, y3p_r, YP)

    def y_down():
        ex[2].wait_recv()
        hop["y2m"].wait_recv()
        total = col_part[2] + ex_r[2].astype(F32)
        y3m_s[0:2] = total[0:2].astype(BF16)
        y3m_s[2:4] = (total[2:4] + y2m_r[...].astype(F32)).astype(BF16)
        hop["y3m"] = send(y3m_s, y3m_r, YM)

    def x_far():
        x2p_s[...] = row_part[xx(2), 0].astype(BF16)
        x2m_s[...] = row_part[xx(2), 1].astype(BF16)
        hop["x2p"] = send(x2p_s, x2p_r, XP)
        hop["x2m"] = send(x2m_s, x2m_r, XM)

    def x_up():
        hop["x2p"].wait_recv()
        x3p_s[0] = (row_part[xx(1), 0] + x2p_r[...].astype(F32)).astype(BF16)
        x3p_s[1] = row_part[xx(1), 1].astype(BF16)
        hop["x3p"] = send(x3p_s, x3p_r, XP)

    def x_down():
        hop["x2m"].wait_recv()
        x3m_s[0] = row_part[xx(3), 0].astype(BF16)
        x3m_s[1] = (row_part[xx(3), 1] + x2m_r[...].astype(F32)).astype(BF16)
        hop["x3m"] = send(x3m_s, x3m_r, XM)

    tiles = [(s, i) for s in range(NY) for i in range(NX)]
    total_tiles = len(tiles)
    for t in range(total_tiles + 2):
        if t < total_tiles:
            score(*tiles[t])
        if 1 <= t <= total_tiles:
            elem(*tiles[t - 1])
        if t >= 2:
            s, i = tiles[t - 2]
            row_grad(s, i)
            if i == NX - 1:
                ex[s] = col_grad(s)
            if (s, i) == (2, 0):
                y_far()
            if (s, i) == (3, 0):
                x_far()
                y_up()
            if (s, i) == (3, 2):
                y_down()
            if (s, i) == (3, 3):
                x_up()
                x_down()

    ex[3].wait_recv()
    hop["y3p"].wait_recv()
    hop["y3m"].wait_recv()
    q_sum[...] = (col_part[3] + ex_r[3].astype(F32)) + (
        y3p_r[...].astype(F32) + y3m_r[...].astype(F32)
    )
    z2p_s[...] = q_sum[zz(2), 0:32].astype(BF16)
    z2m_s[...] = q_sum[zz(2), 32:64].astype(BF16)
    z2p, z2m = send(z2p_s, z2p_r, ZP), send(z2m_s, z2m_r, ZM)
    hop["x3p"].wait_recv()
    hop["x3m"].wait_recv()
    w_s[...] = (
        row_part[x, 1 - zl] + (x3p_r[1 - zl].astype(F32) + x3m_r[1 - zl].astype(F32))
    ).astype(BF16)
    w = send(w_s, w_r, LO)
    z2p.wait_recv()
    z3p_s[0:32] = (q_sum[zz(1), 0:32] + z2p_r[...].astype(F32)).astype(BF16)
    z3p_s[32:64] = q_sum[zz(1), 32:64].astype(BF16)
    z3p = send(z3p_s, z3p_r, ZP)
    z2m.wait_recv()
    z3m_s[0:32] = q_sum[zz(3), 0:32].astype(BF16)
    z3m_s[32:64] = (q_sum[zz(3), 32:64] + z2m_r[...].astype(F32)).astype(BF16)
    z3m = send(z3m_s, z3m_r, ZM)
    for cp in l_acc:
        cp.wait()

    def update(emb, acc, grad, new_ref, acc_ref):
        acc_new = acc + grad * grad
        acc_ref[...] = acc_new
        new_ref[...] = emb - LEARN_RATE * grad / jnp.sqrt(acc_new)

    own = row_part[x, zl] + (x3p_r[zl].astype(F32) + x3m_r[zl].astype(F32))
    w.wait_recv()
    update(remb[...], racc[...], (own + w_r[...].astype(F32)) * (1 / 256), rnew_ref, raccn_ref)
    z3p.wait_recv()
    z3m.wait_recv()
    total = q_sum[zh] + (z3p_r[...].astype(F32) + z3m_r[...].astype(F32))
    update(cemb[...], cacc[...], total * (1 / 128), cnew_ref, caccn_ref)
    for cp in copies:
        cp.wait_send()


def local(counts, row_ids, col_ids, row_marginal, col_marginal, row_emb, row_acc, col_emb, col_acc):
    any_spec = pl.BlockSpec(memory_space=pl.ANY)
    vmem = pltpu.VMEM
    i32 = jnp.int32
    scratch = [
        vmem((ROWS, COLS), i32), vmem((1, ROWS), i32), vmem((1, COLS), i32),
        vmem((320, 128), i32), vmem((128, 128), i32),
        vmem((RB, K), F32), vmem((RB, K), F32), vmem((CB, K), F32), vmem((CB, K), F32),
        vmem((NX, NZL, RB, K), BF16), vmem((K, ROWS), BF16),
        vmem((NY, NZH, NC, CB, K), BF16), vmem((NY, K, QB), BF16),
        vmem((ROWS, 128), F32), vmem((SUB, COLS), F32),
        vmem((2, XB, QB), F32), vmem((2, ROWS, QB), BF16),
        vmem((NX, NZL, RB, K), F32), vmem((2, NZH, NC, CB, K), F32),
        vmem((NY, NZH, CB, K), F32), vmem((NZH, CB, K), F32),
    ]
    scratch += [vmem((NY, NZH, CB, K), BF16)] * 2
    scratch += [vmem((2, CB, K), BF16)] * 4
    scratch += [vmem((4, CB, K), BF16)] * 4
    scratch += [vmem((32, K), BF16)] * 4
    scratch += [vmem((CB, K), BF16)] * 4
    scratch += [vmem((RB, K), BF16)] * 4
    scratch += [vmem((NZL, RB, K), BF16)] * 4
    scratch += [vmem((RB, K), BF16)] * 2
    scratch += [
        pltpu.SemaphoreType.DMA((12,)),
        pltpu.SemaphoreType.DMA((N_SEMS,)),
        pltpu.SemaphoreType.DMA((N_SEMS,)),
    ]
    row_out = jax.ShapeDtypeStruct((RB, K), F32)
    col_out = jax.ShapeDtypeStruct((CB, K), F32)
    return pl.pallas_call(
        kernel,
        out_shape=(row_out, row_out, col_out, col_out),
        in_specs=[any_spec] * 9,
        out_specs=(pl.BlockSpec(memory_space=pltpu.VMEM),) * 4,
        scratch_shapes=scratch,
        compiler_params=pltpu.CompilerParams(
            collective_id=0, has_side_effects=True, vmem_limit_bytes=48 * 1024 * 1024
        ),
        name="step",
    )(
        counts,
        row_ids.reshape(1, ROWS),
        col_ids.reshape(1, COLS),
        row_marginal.reshape(320, 128),
        col_marginal.reshape(128, 128),
        row_emb, row_acc, col_emb, col_acc,
    )


def solution(mesh):
    placed = (
        P("gr", "gc"),
        P("gr"),
        P("gc"),
        P(),
        P(),
        P(("gr", "gc"), None),
        P(("gr", "gc"), None),
        P(("gc", "gr"), None),
        P(("gc", "gr"), None),
    )
    return jax.shard_map(
        local,
        mesh=mesh,
        in_specs=placed,
        out_specs=(
            P(("gr", "gc"), None),
            P(("gr", "gc"), None),
            P(("gc", "gr"), None),
            P(("gc", "gr"), None),
        ),
        check_vma=False,
    )
```

time: 476 us -> 59.8 us (0.13)
  the two profiles are of different devices: /device:TPU:1 before, /device:TPU:2 now
where the time goes in v1:
time: 59.8 us; the launch traced here: 59.4 us
  Pallas kernels  49.5 us (83%)
  local copies, waits for them, and re-layouts  9.25 us (15%)
  between operations  0.65 us (1%)
    pallas_call x1, Pallas kernels, local(): pl.pallas_call(kernel, out_shape=(row_out, row_out, col_out, col_out), in...  49.5 us
    unnamed x18, local copies, waits for them, and re-layouts  8.55 us

profile of v1, /device:TPU:2, one launch (start us, length us, event | category | flops | bytes accessed | tf_op | source)
XLA Modules:
  0.0 59.4 jit_solution(2218359381357275359)
XLA Ops:
  0.6 0.7 %reshape.20.rid_hbm = s32[1,1280]{1,0:T(1,128)S(1)} reshape(s32[1280]{0:T(1024)} %param.10) | data formatting | bytes 10240 | tf_op jit(solution)/shard_map/reshape | solution.py:383
  1.3 0.0 copy-start
  1.3 0.9 %copy-done = s32[40960]{0:T(1024)S(1)} copy-done((s32[40960]{0:T(1024)S(1)}, s32[40960]{0:T(1024)}, u32[]{:S(2)}) %copy-start) | copy-done | bytes 163864
  2.2 0.0 copy-start.1
  2.3 0.9 %copy-done.1 = f32[160,256]{1,0:T(8,128)S(1)} copy-done((f32[160,256]{1,0:T(8,128)S(1)}, f32[160,256]{1,0:T(8,128)}, u32[]{:S(2)}) %copy-start.1) | copy-done | bytes 163864
  3.2 0.0 copy-start.2
  3.2 0.9 %copy-done.2 = f32[160,256]{1,0:T(8,128)S(1)} copy-done((f32[160,256]{1,0:T(8,128)S(1)}, f32[160,256]{1,0:T(8,128)}, u32[]{:S(2)}) %copy-start.2) | copy-done | bytes 163864
  4.1 0.0 copy-start.3
  4.1 0.8 %copy-done.3 = s32[16384]{0:T(1024)S(1)} copy-done((s32[16384]{0:T(1024)S(1)}, s32[16384]{0:T(1024)}, u32[]{:S(2)}) %copy-start.3) | copy-done | bytes 65560
  4.9 0.0 copy-start.4
  4.9 0.8 %copy-done.4 = f32[64,256]{1,0:T(8,128)S(1)} copy-done((f32[64,256]{1,0:T(8,128)S(1)}, f32[64,256]{1,0:T(8,128)}, u32[]{:S(2)}) %copy-start.4) | copy-done | bytes 65560
  5.8 0.0 copy-start.5
  5.8 0.8 %copy-done.5 = f32[64,256]{1,0:T(8,128)S(1)} copy-done((f32[64,256]{1,0:T(8,128)S(1)}, f32[64,256]{1,0:T(8,128)}, u32[]{:S(2)}) %copy-start.5) | copy-done | bytes 65560
  6.6 0.0 copy-start.6
  6.6 0.7 %copy-done.6 = s32[2048]{0:T(1024)S(1)} copy-done((s32[2048]{0:T(1024)S(1)}, s32[2048]{0:T(1024)}, u32[]{:S(2)}) %copy-start.6) | copy-done | bytes 8216
  7.3 49.5 %step.1 = (f32[160,256]{1,0:T(8,128)S(1)}, f32[160,256]{1,0:T(8,128)S(1)}, f32[64,256]{1,0:T(8,128)S(1)}, f32[64,256]{1,0:T(8,128)S(1)}) custom-call(s32[1280,2048]{1,0:T(8,128)} %cnt_hbm.1, s32[1,1280]{1,0:T(1,128)S(1)} %reshape.20.rid_hbm, s32[1,2048]{1,0:T(1,128)S(1)} %bitcast.5, s32[320,128]{1,0:T(8,128)S(1)} %bitcast.3, s32[128,128]{1,0:T(8,128)S(1)} %bitcast.4, ...), custom_call_target="tpu_custom_call" | custom-call | tf_op jit(solution)/shard_map/step/pallas_call | solution.py:371
  56.8 0.7 %copy.17 = f32[160,256]{1,0:T(8,128)} copy(f32[160,256]{1,0:T(8,128)S(1)} %get-tuple-element.8) | data formatting | bytes 327680
  57.5 0.7 %copy.18 = f32[160,256]{1,0:T(8,128)} copy(f32[160,256]{1,0:T(8,128)S(1)} %get-tuple-element.9) | data formatting | bytes 327680
  58.2 0.6 %copy.19 = f32[64,256]{1,0:T(8,128)} copy(f32[64,256]{1,0:T(8,128)S(1)} %get-tuple-element.10) | data formatting | bytes 131072
  58.8 0.6 %copy.20 = f32[64,256]{1,0:T(8,128)} copy(f32[64,256]{1,0:T(8,128)S(1)} %get-tuple-element.11) | data formatting | bytes 131072
Async XLA Ops:
  1.3 0.9 %copy-start = (s32[40960]{0:T(1024)S(1)}, s32[40960]{0:T(1024)}, u32[]{:S(2)}) copy-start(s32[40960]{0:T(1024)} %param.12) | copy-start | bytes 491524
  2.2 0.9 %copy-start.1 = (f32[160,256]{1,0:T(8,128)S(1)}, f32[160,256]{1,0:T(8,128)}, u32[]{:S(2)}) copy-start(f32[160,256]{1,0:T(8,128)} %remb_hbm.1) | copy-start | bytes 491524
  3.2 0.9 %copy-start.2 = (f32[160,256]{1,0:T(8,128)S(1)}, f32[160,256]{1,0:T(8,128)}, u32[]{:S(2)}) copy-start(f32[160,256]{1,0:T(8,128)} %racc_hbm.1) | copy-start | bytes 491524
  4.1 0.8 %copy-start.3 = (s32[16384]{0:T(1024)S(1)}, s32[16384]{0:T(1024)}, u32[]{:S(2)}) copy-start(s32[16384]{0:T(1024)} %param.13) | copy-start | bytes 196612
  4.9 0.8 %copy-start.4 = (f32[64,256]{1,0:T(8,128)S(1)}, f32[64,256]{1,0:T(8,128)}, u32[]{:S(2)}) copy-start(f32[64,256]{1,0:T(8,128)} %cemb_hbm.1) | copy-start | bytes 196612
  5.8 0.8 %copy-start.5 = (f32[64,256]{1,0:T(8,128)S(1)}, f32[64,256]{1,0:T(8,128)}, u32[]{:S(2)}) copy-start(f32[64,256]{1,0:T(8,128)} %cacc_hbm.1) | copy-start | bytes 196612
  6.6 0.7 %copy-start.6 = (s32[2048]{0:T(1024)S(1)}, s32[2048]{0:T(1024)}, u32[]{:S(2)}) copy-start(s32[2048]{0:T(1024)} %param.11) | copy-start | bytes 24580

commit v2 on v1

v2 whole, which is shorter than its diff:
```python
import functools

import jax
import jax.numpy as jnp
from jax import lax
from jax.experimental import pallas as pl
from jax.experimental.pallas import tpu as pltpu
from jax.sharding import PartitionSpec as P

F32 = jnp.float32
BF16 = jnp.bfloat16
MESH = pl.DeviceIdType.MESH

LEARN_RATE = 0.5
K = 256
NX, NZL = 4, 2
NZH, NY, NC = 4, 4, 2
RB = 160
CB = 64
XB = RB * NZL
QB = NZH * NC * CB
ROWS = NX * XB
COLS = NY * QB
SUB = 16
TILES = (
    (1, 0), (3, 0), (0, 1), (1, 1), (3, 1), (0, 3), (1, 3), (3, 3),
    (2, 1), (2, 3), (2, 2), (2, 0), (1, 2), (3, 2), (0, 2), (0, 0),
)
N_SEMS = 64


def lookup(table, ids):
    high = lax.shift_right_logical(ids, 7)
    low = ids & 127
    n_high, n = table.shape[0], ids.shape[1]
    hot = (lax.broadcasted_iota(jnp.int32, (n_high, n), 0) == high).astype(F32).astype(BF16)
    digits = [
        lax.shift_right_logical(table, 16),
        lax.shift_right_logical(table, 8) & 255,
        table & 255,
    ]
    parts = [
        jnp.dot(d.astype(F32).T.astype(BF16), hot, preferred_element_type=F32) for d in digits
    ]
    whole = parts[0] * 65536.0 + parts[1] * 256.0 + parts[2]
    mine = lax.broadcasted_iota(jnp.int32, (128, n), 0) == low
    return jnp.log(jnp.sum(jnp.where(mine, whole, 0.0), axis=0, keepdims=True))


def kernel(
    cnt_hbm, rid_hbm, cid_hbm, rmar_hbm, cmar_hbm, remb_hbm, racc_hbm, cemb_hbm, cacc_hbm,
    rnew_ref, raccn_ref, cnew_ref, caccn_ref,
    cnt, rid, cid, rmar, cmar, remb, racc, cemb, cacc,
    rows, rows_t, cols, cols_t, row_term, col_term,
    s_ref, g_ref, row_part, col_tmp, col_part,
    ex_s, ex_r, col_s, y_r, z_r, far_s, far_r, row_s, row_r, w_s, w_r,
    local_sem, send_sem, recv_sem,
):
    gr = lax.axis_index("gr")
    gc = lax.axis_index("gc")
    c = lax.rem(gr, NC)
    y = lax.rem(gr // NC, NY)
    zh = gr // (NC * NY)
    zl = lax.rem(gc, NZL)
    x = gc // NZL

    def at(dx=0, dzl=0, dzh=0, dy=0, dc=0):
        g = (lax.rem(zh + dzh, NZH) * NY + lax.rem(y + dy, NY)) * NC + lax.rem(c + dc, NC)
        k = lax.rem(x + dx, NX) * NZL + lax.rem(zl + dzl, NZL)
        return (g, k)

    XP, XM, CO, LO = at(dx=1), at(dx=3), at(dc=1), at(dzl=1)
    neighbours = [at(dzh=j) for j in (2, 1, 3)] + [at(dy=d) for d in (2, 1, 3)]
    neighbours += [at(dx=2), XP, XM, LO, CO]

    loads = []

    def load(src, dst):
        cp = pltpu.make_async_copy(src, dst, local_sem.at[len(loads)])
        cp.start()
        loads.append(cp)
        return cp

    l_remb, l_cemb = load(remb_hbm, remb), load(cemb_hbm, cemb)
    barrier = pltpu.get_barrier_semaphore()
    for n in neighbours:
        pl.semaphore_signal(barrier, inc=1, device_id=n, device_id_type=MESH)
    l_ids = [load(rid_hbm, rid), load(cid_hbm, cid), load(rmar_hbm, rmar), load(cmar_hbm, cmar)]
    l_cnt = [
        load(cnt_hbm.at[pl.ds(i * XB, XB)], cnt.at[pl.ds(i * XB, XB)]) for i in range(NX)
    ]
    l_acc = [load(racc_hbm, racc), load(cacc_hbm, cacc)]

    copies = []

    def send(src, dst, target):
        i = len(copies)
        cp = pltpu.make_async_remote_copy(
            src_ref=src, dst_ref=dst, send_sem=send_sem.at[i], recv_sem=recv_sem.at[i],
            device_id=target, device_id_type=MESH,
        )
        cp.start()
        copies.append(cp)
        return cp

    def zz(d):
        return lax.rem(zh + d, NZH)

    def yy(d):
        return lax.rem(y + d, NY)

    def xx(d):
        return lax.rem(x + d, NX)

    def same(ref, target):
        return send(ref, ref, target)

    l_remb.wait()
    rows[x, zl] = (remb[...] * 0.5).astype(BF16)
    l_cemb.wait()
    cols[y, zh, c] = cemb[...].astype(BF16)
    pl.semaphore_wait(barrier, len(neighbours))

    own_r, own_c = rows.at[x, zl], cols.at[y, zh, c]
    z_in, y_in, core_in, q_in = {}, {}, {}, {}

    def spread(j):
        piece = cols.at[y, zz(NZH - j), c]
        core_in[j] = same(piece, CO)
        for d in (1, 3):
            y_in[j, d] = same(piece, at(dy=d))

    for j in (1, 3, 2):
        z_in[j] = same(own_c, at(dzh=j))
    r_lo = same(own_r, LO)
    r_p0, r_m0 = same(own_r, XP), same(own_r, XM)
    spread(0)

    for cp in l_ids:
        cp.wait()
    col_log = lookup(cmar[...], cid[...])
    col_term[...] = jnp.broadcast_to(0.5 * col_log, col_term.shape)
    r_lo.wait_recv()
    other_r = rows.at[x, 1 - zl]
    r_p1, r_m1 = same(other_r, XP), same(other_r, XM)
    for j in (1, 3):
        z_in[j].wait_recv()
        spread(j)
    r_p0.wait_recv()
    r_fp = same(rows.at[xx(3), zl, pl.ds(0, RB // 2)], XP)
    r_m0.wait_recv()
    r_fm = same(rows.at[xx(1), zl, pl.ds(RB // 2, RB // 2)], XM)
    z_in[2].wait_recv()
    spread(2)
    for j in range(NZH):
        y_in[j, 2] = same(cols.at[y, zz(NZH - j), c], at(dy=2))
    row_log = lookup(rmar[...], rid[...].reshape(1, ROWS))
    log_total = jnp.log(jnp.sum(rmar[...].astype(F32)))
    row_vec = 0.5 * (row_log - log_total)
    for b in range(ROWS // 128):
        piece = jnp.broadcast_to(row_vec[:, b * 128 : (b + 1) * 128], (128, 128))
        row_term[b * 128 : (b + 1) * 128, :] = piece.T
    rest = {}

    def rows_ready(dx):
        rows_t[:, dx * XB : (dx + 1) * XB] = rows[xx(dx)].reshape(XB, K).T

    def cols_ready(e):
        cols_t[e] = cols[yy(e)].reshape(QB, K).T

    def cols_to_core(e):
        for j in range(NZH):
            y_in[j, NY - e].wait_recv()
        q_in[e] = same(cols.at[yy(e), :, c], CO)

    def before(t):
        if t == 0:
            rows_ready(0)
            for j in range(NZH):
                core_in[j].wait_recv()
            cols_ready(0)
            r_m1.wait_recv()
            rows_ready(1)
            for cp in l_cnt:
                cp.wait()
        if t == 1:
            r_p1.wait_recv()
            rows_ready(3)
            r_fp.wait_recv()
            r_fm.wait_recv()
            rest["r_lo2"] = same(rows.at[xx(2), zl], LO)
        if t == 2:
            cols_to_core(1)
            cols_to_core(3)
            q_in[1].wait_recv()
            cols_ready(1)
        if t == 4:
            cols_to_core(2)
        if t == 5:
            q_in[3].wait_recv()
            cols_ready(3)
        if t == 8:
            rest["r_lo2"].wait_recv()
            rows_ready(2)
        if t == 10:
            q_in[2].wait_recv()
            cols_ready(2)

    def score(t):
        dx, e = TILES[t]
        s_ref[t % 2] = jnp.dot(
            rows[xx(dx)].reshape(XB, K), cols_t[e], preferred_element_type=F32
        )

    def elem(t):
        dx, e = TILES[t]
        r_at = pl.multiple_of(xx(dx) * XB, XB)
        for z in range(NZH):
            c_at = pl.multiple_of(z * QB + yy(e) * 128, 128)
            c_row = col_term[:, pl.ds(c_at, 128)]
            for u in range(XB // SUB):
                at_u = pl.ds(pl.multiple_of(r_at + u * SUB, SUB), SUB)
                n = cnt[at_u, pl.ds(c_at, 128)]
                m = jnp.maximum(n, 1).astype(F32)
                inv = lax.rsqrt(m)
                half = (
                    s_ref[t % 2, u * SUB : (u + 1) * SUB, z * 128 : (z + 1) * 128] + jnp.log(inv)
                ) + (row_term[at_u, :] + c_row)
                g = jnp.where(n > 0, (m * inv + 0.4) * half, jnp.tanh(half) + 1.0)
                at_g = dx * XB + u * SUB
                g_ref[e, at_g : at_g + SUB, z * 128 : (z + 1) * 128] = g.astype(BF16)

    def row_grad(t):
        dx, e = TILES[t]
        part = jnp.dot(
            g_ref[e, dx * XB : (dx + 1) * XB, :],
            cols[yy(e)].reshape(QB, K),
            preferred_element_type=F32,
        ).reshape(NZL, RB, K)
        if dx not in [a for a, _ in TILES[:t]]:
            row_part[dx] = part
        else:
            row_part[dx] += part

    ex, row_in = {}, {}

    def col_grad(e):
        t = jnp.dot(rows_t[...], g_ref[e], preferred_element_type=F32)
        col_tmp[e] = t.T.reshape(NZH, NC, CB, K)
        ex_s[e] = col_tmp[e, :, 1 - c].astype(BF16)
        ex[e] = send(ex_s.at[e], ex_r.at[e], CO)

    y_back, z_back = {}, {}

    def col_out(e):
        ex[e].wait_recv()
        total = col_tmp[e, :, c] + ex_r[e].astype(F32)
        if e == 0:
            for d in (1, 3):
                y_back[d].wait_recv()
                total = total + y_r[d // 2].astype(F32)
        col_s[e] = total.astype(BF16)
        if e % 2:
            y_back[e] = send(col_s.at[e], y_r.at[e // 2], at(dy=e))
        else:
            col_part[e // 2] = total
            for j in (2, 1, 3):
                z_back[e, j] = send(col_s.at[e, zz(j)], z_r.at[e // 2, j - 1], at(dzh=j))

    def z_sum(e):
        for j in (1, 3, 2):
            z_back[e, j].wait_recv()
        total = col_part[e // 2, zh]
        for j in range(NZH - 1):
            total = total + z_r[e // 2, j].astype(F32)
        return total

    def row_out(dx):
        row_s[dx - 1] = row_part[dx].astype(BF16)
        row_in[dx] = send(row_s.at[dx - 1], row_r.at[dx - 1], at(dx=dx))

    n_tiles = len(TILES)
    for t in range(n_tiles + 2):
        late = t == 2
        if t < n_tiles and not late:
            before(t)
            score(t)
        if 1 <= t <= n_tiles:
            elem(t - 1)
        if t >= 2:
            row_grad(t - 2)
        if late:
            before(t)
            score(t)
        if t == 10:
            col_grad(1)
        if t == 11:
            col_grad(3)
        if t == 13:
            col_out(1)
            row_out(2)
        if t == 14:
            row_out(1)
            col_out(3)
        if t == 15:
            row_out(3)
        if t == 16:
            col_grad(2)
        if t == 17:
            col_grad(0)

    col_out(2)
    col_out(0)
    for dx in (2, 1, 3):
        row_in[dx].wait_recv()

    def row_sum(at_zl):
        total = row_part[0, at_zl]
        for i in range(NX - 1):
            total = total + row_r[i, at_zl].astype(F32)
        return total

    w_s[...] = row_sum(1 - zl).astype(BF16)
    w = send(w_s, w_r, LO)
    far_s[...] = z_sum(2).astype(BF16)
    far = send(far_s, far_r, at(dy=2))
    own = row_sum(zl)
    for cp in l_acc:
        cp.wait()

    def update(emb, acc, grad, new_ref, acc_ref):
        acc_new = acc + grad * grad
        acc_ref[...] = acc_new
        new_ref[...] = emb - LEARN_RATE * grad / jnp.sqrt(acc_new)

    w.wait_recv()
    update(remb[...], racc[...], (own + w_r[...].astype(F32)) * (1 / 256), rnew_ref, raccn_ref)
    total = z_sum(0)
    far.wait_recv()
    total = total + far_r[...].astype(F32)
    update(cemb[...], cacc[...], total * (1 / 128), cnew_ref, caccn_ref)
    for cp in copies:
        cp.wait_send()


def hand_over(*refs):
    n = len(refs) // 2
    sem = refs[-1]
    moves = [pltpu.make_async_copy(refs[i], refs[n + i], sem.at[i]) for i in range(n)]
    for m in moves:
        m.start()
    for m in moves:
        m.wait()


def local(counts, row_ids, col_ids, row_marginal, col_marginal, row_emb, row_acc, col_emb, col_acc):
    hbm = pl.BlockSpec(memory_space=pltpu.HBM)
    vmem = pltpu.VMEM
    i32 = jnp.int32
    scratch = [
        vmem((ROWS, COLS), i32), vmem((ROWS,), i32), vmem((1, COLS), i32),
        vmem((320, 128), i32), vmem((128, 128), i32),
        vmem((RB, K), F32), vmem((RB, K), F32), vmem((CB, K), F32), vmem((CB, K), F32),
        vmem((NX, NZL, RB, K), BF16), vmem((K, ROWS), BF16),
        vmem((NY, NZH, NC, CB, K), BF16), vmem((NY, K, QB), BF16),
        vmem((ROWS, 128), F32), vmem((SUB, COLS), F32),
        vmem((2, XB, QB), F32), vmem((NY, ROWS, QB), BF16),
        vmem((NX, NZL, RB, K), F32), vmem((NY, NZH, NC, CB, K), F32), vmem((2, NZH, CB, K), F32),
        vmem((NY, NZH, CB, K), BF16), vmem((NY, NZH, CB, K), BF16), vmem((NY, NZH, CB, K), BF16),
        vmem((2, NZH, CB, K), BF16), vmem((2, NZH - 1, CB, K), BF16),
        vmem((CB, K), BF16), vmem((CB, K), BF16),
        vmem((NX - 1, NZL, RB, K), BF16), vmem((NX - 1, NZL, RB, K), BF16),
        vmem((RB, K), BF16), vmem((RB, K), BF16),
        pltpu.SemaphoreType.DMA((12,)),
        pltpu.SemaphoreType.DMA((N_SEMS,)),
        pltpu.SemaphoreType.DMA((N_SEMS,)),
    ]
    shapes = ((RB, K), (RB, K), (CB, K), (CB, K))
    operands = (
        counts, row_ids, col_ids.reshape(1, COLS),
        row_marginal.reshape(320, 128), col_marginal.reshape(128, 128),
        row_emb, row_acc, col_emb, col_acc,
    )
    out = pl.pallas_call(
        kernel,
        out_shape=tuple(pltpu.VMEM(s, F32) for s in shapes),
        in_specs=[hbm] * 9,
        out_specs=(pl.BlockSpec(memory_space=pltpu.VMEM),) * 4,
        scratch_shapes=scratch,
        compiler_params=pltpu.CompilerParams(
            collective_id=0, has_side_effects=True, vmem_limit_bytes=48 * 1024 * 1024
        ),
        name="step",
    )(*[pltpu.with_memory_space_constraint(a, pltpu.HBM) for a in operands])
    return pl.pallas_call(
        hand_over,
        out_shape=tuple(jax.ShapeDtypeStruct(s, F32) for s in shapes),
        in_specs=[pl.BlockSpec(memory_space=pltpu.VMEM)] * 4,
        out_specs=(hbm,) * 4,
        scratch_shapes=[pltpu.SemaphoreType.DMA((4,))],
        name="hand_over",
    )(*[pltpu.with_memory_space_constraint(a, pltpu.VMEM) for a in out])


def solution(mesh):
    placed = (
        P("gr", "gc"),
        P("gr"),
        P("gc"),
        P(),
        P(),
        P(("gr", "gc"), None),
        P(("gr", "gc"), None),
        P(("gc", "gr"), None),
        P(("gc", "gr"), None),
    )
    return jax.shard_map(
        local,
        mesh=mesh,
        in_specs=placed,
        out_specs=(
            P(("gr", "gc"), None),
            P(("gr", "gc"), None),
            P(("gc", "gr"), None),
            P(("gc", "gr"), None),
        ),
        check_vma=False,
    )
```

time: 59.8 us -> 45.3 us (0.76)
  the two profiles are of different devices: /device:TPU:2 before, /device:TPU:1 now
where the time goes in v2:
time: 45.3 us
  Pallas kernels  44.6 us (98%)
  between operations  0.64 us (1%)
    pallas_call x1, Pallas kernels, local(): pl.pallas_call(kernel, out_shape=tuple((pltpu.VMEM(s, F32) for s in shape...  43.8 us

profile of v2, /device:TPU:1, one launch (start us, length us, event | category | flops | bytes accessed | tf_op | source)
XLA Modules:
  0.0 45.3 jit_solution(18297516503703091092)
XLA Ops:
  0.6 43.8 %step.1 = (f32[160,256]{1,0:T(8,128)S(1)}, f32[160,256]{1,0:T(8,128)S(1)}, f32[64,256]{1,0:T(8,128)S(1)}, f32[64,256]{1,0:T(8,128)S(1)}) custom-call(s32[1280,2048]{1,0:T(8,128)} %cnt_hbm.1, s32[1280]{0:T(1024)} %rid_hbm.1, s32[1,2048]{1,0:T(1,128)} %bitcast.5, s32[320,128]{1,0:T(8,128)} %bitcast.3, s32[128,128]{1,0:T(8,128)} %bitcast.4, ...), custom_call_target="tpu_custom_call" | custom-call | tf_op jit(solution)/shard_map/step/pallas_call | solution.py:384
  44.5 0.8 %hand_over.1 = (f32[160,256]{1,0:T(8,128)}, f32[160,256]{1,0:T(8,128)}, f32[64,256]{1,0:T(8,128)}, f32[64,256]{1,0:T(8,128)}) custom-call(f32[160,256]{1,0:T(8,128)S(1)} %get-tuple-element.8.refs_0_, f32[160,256]{1,0:T(8,128)S(1)} %get-tuple-element.9.refs_1_, f32[64,256]{1,0:T(8,128)S(1)} %get-tuple-element.10.refs_2_, f32[64,256]{1,0:T(8,128)S(1)} %get-tuple-element.11.refs_3_), custom_call_target="tpu_custom_call" | custom-call | tf_op jit(solution)/shard_map/hand_over/pallas_call | solution.py:395

commit v3 on v2

v3 whole, which is shorter than its diff:
```python
import functools

import jax
import jax.numpy as jnp
from jax import lax
from jax.experimental import pallas as pl
from jax.experimental.pallas import tpu as pltpu
from jax.sharding import PartitionSpec as P

F32 = jnp.float32
BF16 = jnp.bfloat16
MESH = pl.DeviceIdType.MESH

LEARN_RATE = 0.5
K = 256
NX, NZL = 4, 2
NZH, NY, NC = 4, 4, 2
RB = 160
CB = 64
XB = RB * NZL
QB = NY * NC * CB
ROWS = NX * XB
COLS = NZH * QB
SUB = 16
TILES = (
    (0, 0), (3, 0), (1, 0), (2, 0), (0, 1), (3, 1), (1, 1), (2, 1),
    (0, 2), (3, 2), (1, 2), (2, 2), (2, 3), (1, 3), (3, 3), (0, 3),
)
LATE = (1, 3, 4, 8, 12)
SPREAD = {1: 2, 2: 3}
FORWARD = {3: (1,), 6: (2,), 9: (3,)}
PIECES = (2, 1, 3, 0)
N_SEMS = 80


def lookup(table, ids):
    high = lax.shift_right_logical(ids, 7)
    low = ids & 127
    n_high, n = table.shape[0], ids.shape[1]
    hot = (lax.broadcasted_iota(jnp.int32, (n_high, n), 0) == high).astype(F32).astype(BF16)
    digits = [
        lax.shift_right_logical(table, 16),
        lax.shift_right_logical(table, 8) & 255,
        table & 255,
    ]
    parts = [
        jnp.dot(d.astype(F32).T.astype(BF16), hot, preferred_element_type=F32) for d in digits
    ]
    whole = parts[0] * 65536.0 + parts[1] * 256.0 + parts[2]
    mine = lax.broadcasted_iota(jnp.int32, (128, n), 0) == low
    return jnp.log(jnp.sum(jnp.where(mine, whole, 0.0), axis=0, keepdims=True))


def kernel(
    cnt_hbm, rid_hbm, cid_hbm, rmar_hbm, cmar_hbm, remb_hbm, racc_hbm, cemb_hbm, cacc_hbm,
    rnew_ref, raccn_ref, cnew_ref, caccn_ref,
    cnt, rid, cid, rmar, cmar, remb, racc, cemb, cacc,
    rows, rows_t, cols, row_term, col_term,
    s_ref, g_ref, row_part, col_tmp, col_part,
    ex_s, ex_r, col_s, y_r, z_s, z_r, row_s, row_r, w_s, w_r,
    local_sem, send_sem, recv_sem, z_send, z_recv, sum_send, sum_recv, here,
):
    gr = lax.axis_index("gr")
    gc = lax.axis_index("gc")
    c = lax.rem(gr, NC)
    y = lax.rem(gr // NC, NY)
    zh = gr // (NC * NY)
    zl = lax.rem(gc, NZL)
    x = gc // NZL

    def at(dx=0, dzl=0, dzh=0, dy=0, dc=0):
        g = (lax.rem(zh + dzh, NZH) * NY + lax.rem(y + dy, NY)) * NC + lax.rem(c + dc, NC)
        k = lax.rem(x + dx, NX) * NZL + lax.rem(zl + dzl, NZL)
        return (g, k)

    XP, XM, CO, LO = at(dx=1), at(dx=3), at(dc=1), at(dzl=1)
    neighbours = [at(dy=d) for d in (2, 1, 3)] + [at(dx=2), XP, XM, LO, CO]

    def z_device(to):
        return ((to * NY + y) * NC + c, gc)

    place = [zh] + [jnp.where(zh <= i, i + 1, i) for i in range(NZH - 1)]

    loads = []

    def load(src, dst):
        cp = pltpu.make_async_copy(src, dst, local_sem.at[len(loads)])
        cp.start()
        loads.append(cp)
        return cp

    l_remb, l_cemb = load(remb_hbm, remb), load(cemb_hbm, cemb)
    barrier = pltpu.get_barrier_semaphore()
    for n in neighbours:
        pl.semaphore_signal(barrier, inc=1, device_id=n, device_id_type=MESH)
    for to in range(1, NZH):

        @pl.when(zh < to)
        def _(to=to):
            pl.semaphore_signal(barrier, inc=1, device_id=z_device(to), device_id_type=MESH)

    l_ids = [load(rid_hbm, rid), load(cid_hbm, cid), load(rmar_hbm, rmar), load(cmar_hbm, cmar)]
    l_cnt = [
        load(cnt_hbm.at[pl.ds(i * XB, XB)], cnt.at[pl.ds(i * XB, XB)]) for i in range(NX)
    ]
    l_acc = [load(racc_hbm, racc), load(cacc_hbm, cacc)]

    copies = []

    def send(src, dst, target):
        i = len(copies)
        cp = pltpu.make_async_remote_copy(
            src_ref=src, dst_ref=dst, send_sem=send_sem.at[i], recv_sem=recv_sem.at[i],
            device_id=target, device_id_type=MESH,
        )
        cp.start()
        copies.append(cp)
        return cp

    def yy(d):
        return lax.rem(y + d, NY)

    def xx(d):
        return lax.rem(x + d, NX)

    def same(ref, target):
        return send(ref, ref, target)

    l_remb.wait()
    rows[x, zl] = (remb[...] * 0.5).astype(BF16)
    l_cemb.wait()
    cols[zh, y, c] = cemb[...].astype(BF16)
    pl.semaphore_wait(barrier, len(neighbours) + zh)

    own_r, own_c = rows.at[x, zl], cols.at[zh, y, c]
    y_in, core_in = {}, {}

    def z_copy(to):
        return pltpu.make_async_remote_copy(
            src_ref=own_c, dst_ref=own_c, send_sem=z_send.at[to], recv_sem=z_recv.at[zh],
            device_id=z_device(to), device_id_type=MESH,
        )

    for to in range(NZH - 1):

        @pl.when(zh > to)
        def _(to=to):
            pl.semaphore_signal(
                here.at[zh], inc=1, device_id=z_device(to), device_id_type=MESH
            )
            z_copy(to).start()

    def spread(b):
        piece = cols.at[place[b], y, c]
        if b:
            pltpu.make_async_remote_copy(
                src_ref=piece, dst_ref=piece, send_sem=z_send.at[place[b]],
                recv_sem=z_recv.at[place[b]], device_id=z_device(place[b]), device_id_type=MESH,
            ).wait_recv()
        core_in[b, 0] = same(piece, CO)
        for d in (1, 3, 2):
            y_in[b, d] = same(piece, at(dy=d))

    def cols_to_core(b):
        for d in (1, 3, 2):
            y_in[b, d].wait_recv()
            core_in[b, d] = same(cols.at[place[b], yy(NY - d), c], CO)

    spread(0)
    r_lo = same(own_r, LO)
    r_p0, r_m0, r_x2 = same(own_r, XP), same(own_r, XM), same(own_r, at(dx=2))

    for cp in l_ids:
        cp.wait()
    col_log = lookup(cmar[...], cid[...])
    col_term[...] = jnp.broadcast_to(0.5 * col_log, col_term.shape)
    r_lo.wait_recv()
    other_r = rows.at[x, 1 - zl]
    r_p1, r_m1 = same(other_r, XP), same(other_r, XM)
    for to in range(1, NZH):

        @pl.when(zh < to)
        def _(to=to):
            pl.semaphore_wait(here.at[to], 1)
            z_copy(to).start()

    spread(1)
    r_x2.wait_recv()
    r_lo2 = same(rows.at[xx(2), zl], LO)
    cols_to_core(0)
    row_log = lookup(rmar[...], rid[...].reshape(1, ROWS))
    log_total = jnp.log(jnp.sum(rmar[...].astype(F32)))
    row_vec = 0.5 * (row_log - log_total)
    for b in range(ROWS // 128):
        piece = jnp.broadcast_to(row_vec[:, b * 128 : (b + 1) * 128], (128, 128))
        row_term[b * 128 : (b + 1) * 128, :] = piece.T
    def rows_ready(dx):
        rows_t[:, dx * XB : (dx + 1) * XB] = rows[xx(dx)].reshape(XB, K).T

    def cols_ready(b):
        for d in range(NY):
            core_in[b, d].wait_recv()

    def before(t):
        dx, e = TILES[t]
        if t in SPREAD:
            spread(SPREAD[t])
        for b in FORWARD.get(t, ()):
            cols_to_core(b)
        if dx not in [a for a, _ in TILES[:t]]:
            for cp in {0: (), 1: (r_m0, r_m1), 2: (r_lo2,), 3: (r_p0, r_p1)}[dx]:
                cp.wait_recv()
            rows_ready(dx)
        if e not in [a for _, a in TILES[:t]]:
            cols_ready(e)
        if t == 0:
            for cp in l_cnt:
                cp.wait()

    def score(t):
        dx, e = TILES[t]
        s_ref[t % 2] = jnp.dot(
            rows[xx(dx)].reshape(XB, K), cols[place[e]].reshape(QB, K).T, preferred_element_type=F32
        )

    def elem(t):
        dx, e = TILES[t]
        r_at = pl.multiple_of(xx(dx) * XB, XB)
        for z in range(QB // 128):
            c_at = pl.multiple_of(place[e] * QB + z * 128, 128)
            c_row = col_term[:, pl.ds(c_at, 128)]
            for u in range(XB // SUB):
                at_u = pl.ds(pl.multiple_of(r_at + u * SUB, SUB), SUB)
                n = cnt[at_u, pl.ds(c_at, 128)]
                m = jnp.maximum(n, 1).astype(F32)
                inv = lax.rsqrt(m)
                half = (
                    s_ref[t % 2, u * SUB : (u + 1) * SUB, z * 128 : (z + 1) * 128] + jnp.log(inv)
                ) + (row_term[at_u, :] + c_row)
                g = jnp.where(n > 0, (m * inv + 0.4) * half, jnp.tanh(half) + 1.0)
                at_g = dx * XB + u * SUB
                g_ref[e, at_g : at_g + SUB, z * 128 : (z + 1) * 128] = g.astype(BF16)

    def row_grad(t):
        dx, e = TILES[t]
        part = jnp.dot(
            g_ref[e, dx * XB : (dx + 1) * XB, :],
            cols[place[e]].reshape(QB, K),
            preferred_element_type=F32,
        ).reshape(NZL, RB, K)
        if dx not in [a for a, _ in TILES[:t]]:
            row_part[dx] = part
        else:
            row_part[dx] += part

    ex, row_in = {}, {}

    def col_grad(e):
        t = jnp.dot(rows_t[...], g_ref[e], preferred_element_type=F32)
        col_tmp[e] = t.T.reshape(NY, NC, CB, K)
        for d in PIECES:
            ex_s[e, yy(d)] = col_tmp[e, yy(d), 1 - c].astype(BF16)
            ex[e, d] = send(ex_s.at[e, yy(d)], ex_r.at[e, yy(d)], CO)

    y_back, z_back = {}, {}

    def both_cores(e, d):
        ex[e, d].wait_recv()
        return col_tmp[e, yy(d), c] + ex_r[e, yy(d)].astype(F32)

    def col_out(e):
        for d in PIECES:
            if d:
                col_s[e, d - 1] = both_cores(e, d).astype(BF16)
                y_back[e, d] = send(col_s.at[e, d - 1], y_r.at[e, d - 1], at(dy=d))
            else:
                col_part[e] = both_cores(e, d)

    def sum_copy(e):
        return pltpu.make_async_remote_copy(
            src_ref=z_s.at[e - 1], dst_ref=z_r.at[zh], send_sem=sum_send.at[e],
            recv_sem=sum_recv.at[zh], device_id=z_device(place[e]), device_id_type=MESH,
        )

    def sum_in(e):
        pltpu.make_async_remote_copy(
            src_ref=z_s.at[e - 1], dst_ref=z_r.at[place[e]], send_sem=sum_send.at[e],
            recv_sem=sum_recv.at[place[e]], device_id=z_device(place[e]), device_id_type=MESH,
        ).wait_recv()

    def col_sum(e):
        total = col_part[e]
        for d in (1, 3, 2):
            y_back[e, d].wait_recv()
            total = total + y_r[e, d - 1].astype(F32)
        if e:
            z_s[e - 1] = total.astype(BF16)
            z_back[e] = sum_copy(e)
            z_back[e].start()
        else:
            col_part[0] = total

    def row_out(dx):
        for p in (1, 0):
            at_zl = lax.rem(zl + p, NZL)
            row_s[dx - 1, at_zl] = row_part[dx, at_zl].astype(BF16)
            row_in[dx, p] = send(row_s.at[dx - 1, at_zl], row_r.at[dx - 1, at_zl], at(dx=dx))

    n_tiles = len(TILES)
    row_end = {dx: max(i for i in range(n_tiles) if TILES[i][0] == dx) for dx in range(NX)}
    col_end = {e: max(i for i in range(n_tiles) if TILES[i][1] == e) for e in range(NZH)}
    col_order = sorted(range(NZH), key=col_end.get)
    for t in range(n_tiles + 2):
        late = t in LATE
        if t < n_tiles and not late:
            before(t)
            score(t)
        if 1 <= t <= n_tiles:
            elem(t - 1)
        if t >= 2:
            row_grad(t - 2)
        if late:
            before(t)
            score(t)
        for dx in range(1, NX):
            if t == row_end[dx] + 2:
                row_out(dx)
        for e in range(NZH):
            if t == col_end[e] + 2:
                col_grad(e)
        for e in col_order:
            if t == col_end[e] + 4:
                col_out(e)
            if t == col_end[e] + 10:
                col_sum(e)

    for e in col_order:
        if col_end[e] + 4 >= n_tiles + 2:
            col_out(e)
    left = [e for e in col_order if col_end[e] + 10 >= n_tiles + 2]
    for e in left[:-1]:
        col_sum(e)

    def row_sum(at_zl):
        total = row_part[0, at_zl]
        for i in range(NX - 1):
            total = total + row_r[i, at_zl].astype(F32)
        return total

    for dx in sorted((1, 2, 3), key=row_end.get):
        row_in[dx, 1].wait_recv()
    w_s[...] = row_sum(1 - zl).astype(BF16)
    w = send(w_s, w_r, LO)
    for e in left[-1:]:
        col_sum(e)
    for dx in (1, 3, 2):
        row_in[dx, 0].wait_recv()
    own = row_sum(zl)
    for cp in l_acc:
        cp.wait()

    def update(emb, acc, grad, new_ref, acc_ref):
        acc_new = acc + grad * grad
        acc_ref[...] = acc_new
        new_ref[...] = emb - LEARN_RATE * grad / jnp.sqrt(acc_new)

    w.wait_recv()
    update(remb[...], racc[...], (own + w_r[...].astype(F32)) * (1 / 256), rnew_ref, raccn_ref)
    total = col_part[0]
    for e in (1, 2, 3):
        sum_in(e)
        total = total + z_r[place[e]].astype(F32)
    update(cemb[...], cacc[...], total * (1 / 128), cnew_ref, caccn_ref)
    for cp in copies:
        cp.wait_send()
    for e in range(1, NZH):
        z_back[e].wait_send()
        z_copy(place[e]).wait_send()


def hand_over(*refs):
    n = len(refs) // 2
    sem = refs[-1]
    moves = [pltpu.make_async_copy(refs[i], refs[n + i], sem.at[i]) for i in range(n)]
    for m in moves:
        m.start()
    for m in moves:
        m.wait()


def local(counts, row_ids, col_ids, row_marginal, col_marginal, row_emb, row_acc, col_emb, col_acc):
    hbm = pl.BlockSpec(memory_space=pltpu.HBM)
    vmem = pltpu.VMEM
    i32 = jnp.int32
    scratch = [
        vmem((ROWS, COLS), i32), vmem((ROWS,), i32), vmem((1, COLS), i32),
        vmem((320, 128), i32), vmem((128, 128), i32),
        vmem((RB, K), F32), vmem((RB, K), F32), vmem((CB, K), F32), vmem((CB, K), F32),
        vmem((NX, NZL, RB, K), BF16), vmem((K, ROWS), BF16),
        vmem((NZH, NY, NC, CB, K), BF16),
        vmem((ROWS, 128), F32), vmem((SUB, COLS), F32),
        vmem((2, XB, QB), F32), vmem((NZH, ROWS, QB), BF16),
        vmem((NX, NZL, RB, K), F32), vmem((NZH, NY, NC, CB, K), F32), vmem((NZH, CB, K), F32),
        vmem((NZH, NY, CB, K), BF16), vmem((NZH, NY, CB, K), BF16),
        vmem((NZH, NY - 1, CB, K), BF16), vmem((NZH, NY - 1, CB, K), BF16),
        vmem((NZH - 1, CB, K), BF16), vmem((NZH, CB, K), BF16),
        vmem((NX - 1, NZL, RB, K), BF16), vmem((NX - 1, NZL, RB, K), BF16),
        vmem((RB, K), BF16), vmem((RB, K), BF16),
        pltpu.SemaphoreType.DMA((12,)),
        pltpu.SemaphoreType.DMA((N_SEMS,)),
        pltpu.SemaphoreType.DMA((N_SEMS,)),
        pltpu.SemaphoreType.DMA((NZH,)),
        pltpu.SemaphoreType.DMA((NZH,)),
        pltpu.SemaphoreType.DMA((NZH,)),
        pltpu.SemaphoreType.DMA((NZH,)),
        pltpu.SemaphoreType.REGULAR((NZH,)),
    ]
    shapes = ((RB, K), (RB, K), (CB, K), (CB, K))
    operands = (
        counts, row_ids, col_ids.reshape(1, COLS),
        row_marginal.reshape(320, 128), col_marginal.reshape(128, 128),
        row_emb, row_acc, col_emb, col_acc,
    )
    out = pl.pallas_call(
        kernel,
        out_shape=tuple(pltpu.VMEM(s, F32) for s in shapes),
        in_specs=[hbm] * 9,
        out_specs=(pl.BlockSpec(memory_space=pltpu.VMEM),) * 4,
        scratch_shapes=scratch,
        compiler_params=pltpu.CompilerParams(
            collective_id=0, has_side_effects=True, vmem_limit_bytes=48 * 1024 * 1024
        ),
        name="step",
    )(*[pltpu.with_memory_space_constraint(a, pltpu.HBM) for a in operands])
    return pl.pallas_call(
        hand_over,
        out_shape=tuple(jax.ShapeDtypeStruct(s, F32) for s in shapes),
        in_specs=[pl.BlockSpec(memory_space=pltpu.VMEM)] * 4,
        out_specs=(hbm,) * 4,
        scratch_shapes=[pltpu.SemaphoreType.DMA((4,))],
        name="hand_over",
    )(*[pltpu.with_memory_space_constraint(a, pltpu.VMEM) for a in out])


def solution(mesh):
    placed = (
        P("gr", "gc"),
        P("gr"),
        P("gc"),
        P(),
        P(),
        P(("gr", "gc"), None),
        P(("gr", "gc"), None),
        P(("gc", "gr"), None),
        P(("gc", "gr"), None),
    )
    return jax.shard_map(
        local,
        mesh=mesh,
        in_specs=placed,
        out_specs=(
            P(("gr", "gc"), None),
            P(("gr", "gc"), None),
            P(("gc", "gr"), None),
            P(("gc", "gr"), None),
        ),
        check_vma=False,
    )
```

time: 45.3 us -> 41.2 us (0.909); the launches traced: 45.3 us -> 40.7 us
  Pallas kernels: 44.6 us -> 40.1 us
    pallas_call x1, Pallas kernels: 43.8 us -> 39.3 us  [local(): pl.pallas_call(kernel, out_shape=tuple((pltpu.VMEM(s, F32) for s in shape...]
where the time goes in v3:
time: 41.2 us; the launch traced here: 40.7 us
  Pallas kernels  40.1 us (97%)
  between operations  0.64 us (2%)
    pallas_call x1, Pallas kernels, local(): pl.pallas_call(kernel, out_shape=tuple((pltpu.VMEM(s, F32) for s in shape...  39.3 us

profile of v3, /device:TPU:1, one launch (start us, length us, event | category | flops | bytes accessed | tf_op | source)
XLA Modules:
  0.0 40.7 jit_solution(2973371535974331662)
XLA Ops:
  0.6 39.3 %step.1 = (f32[160,256]{1,0:T(8,128)S(1)}, f32[160,256]{1,0:T(8,128)S(1)}, f32[64,256]{1,0:T(8,128)S(1)}, f32[64,256]{1,0:T(8,128)S(1)}) custom-call(s32[1280,2048]{1,0:T(8,128)} %cnt_hbm.1, s32[1280]{0:T(1024)} %rid_hbm.1, s32[1,2048]{1,0:T(1,128)} %bitcast.5, s32[320,128]{1,0:T(8,128)} %bitcast.3, s32[128,128]{1,0:T(8,128)} %bitcast.4, ...), custom_call_target="tpu_custom_call" | custom-call | tf_op jit(solution)/shard_map/step/pallas_call | solution.py:424
  39.9 0.8 %hand_over.1 = (f32[160,256]{1,0:T(8,128)}, f32[160,256]{1,0:T(8,128)}, f32[64,256]{1,0:T(8,128)}, f32[64,256]{1,0:T(8,128)}) custom-call(f32[160,256]{1,0:T(8,128)S(1)} %get-tuple-element.8.refs_0_, f32[160,256]{1,0:T(8,128)S(1)} %get-tuple-element.9.refs_1_, f32[64,256]{1,0:T(8,128)S(1)} %get-tuple-element.10.refs_2_, f32[64,256]{1,0:T(8,128)S(1)} %get-tuple-element.11.refs_3_), custom_call_target="tpu_custom_call" | custom-call | tf_op jit(solution)/shard_map/hand_over/pallas_call | solution.py:435

commit v4 on v3

--- a/solution.py
+++ b/solution.py
@@ -100,9 +100,6 @@
             pl.semaphore_signal(barrier, inc=1, device_id=z_device(to), device_id_type=MESH)
 
     l_ids = [load(rid_hbm, rid), load(cid_hbm, cid), load(rmar_hbm, rmar), load(cmar_hbm, cmar)]
-    l_cnt = [
-        load(cnt_hbm.at[pl.ds(i * XB, XB)], cnt.at[pl.ds(i * XB, XB)]) for i in range(NX)
-    ]
     l_acc = [load(racc_hbm, racc), load(cacc_hbm, cacc)]
 
     copies = []
@@ -158,7 +155,7 @@
                 recv_sem=z_recv.at[place[b]], device_id=z_device(place[b]), device_id_type=MESH,
             ).wait_recv()
         core_in[b, 0] = same(piece, CO)
-        for d in (1, 3, 2):
+        for d in (2, 1, 3):
             y_in[b, d] = same(piece, at(dy=d))
 
     def cols_to_core(b):
@@ -170,6 +167,9 @@
     r_lo = same(own_r, LO)
     r_p0, r_m0, r_x2 = same(own_r, XP), same(own_r, XM), same(own_r, at(dx=2))
 
+    l_cnt = [
+        load(cnt_hbm.at[pl.ds(i * XB, XB)], cnt.at[pl.ds(i * XB, XB)]) for i in range(NX)
+    ]
     for cp in l_ids:
         cp.wait()
     col_log = lookup(cmar[...], cid[...])

time: 41.2 us -> 41.3 us (level)
  the two profiles are of different devices: /device:TPU:1 before, /device:TPU:192 now
where the time goes in v4:
time: 41.3 us; the launch traced here: 41.2 us
  Pallas kernels  40.6 us (98%)
  between operations  0.64 us (2%)
    pallas_call x1, Pallas kernels, local(): pl.pallas_call(kernel, out_shape=tuple((pltpu.VMEM(s, F32) for s in shape...  39.8 us

profile of v4, /device:TPU:192, one launch (start us, length us, event | category | flops | bytes accessed | tf_op | source)
XLA Modules:
  0.0 41.2 jit_solution(16710370723317477685)
XLA Ops:
  0.6 39.8 %step.1 = (f32[160,256]{1,0:T(8,128)S(1)}, f32[160,256]{1,0:T(8,128)S(1)}, f32[64,256]{1,0:T(8,128)S(1)}, f32[64,256]{1,0:T(8,128)S(1)}) custom-call(s32[1280,2048]{1,0:T(8,128)} %cnt_hbm.1, s32[1280]{0:T(1024)} %rid_hbm.1, s32[1,2048]{1,0:T(1,128)} %bitcast.5, s32[320,128]{1,0:T(8,128)} %bitcast.3, s32[128,128]{1,0:T(8,128)} %bitcast.4, ...), custom_call_target="tpu_custom_call" | custom-call | tf_op jit(solution)/shard_map/step/pallas_call | solution.py:424
  40.4 0.8 %hand_over.1 = (f32[160,256]{1,0:T(8,128)}, f32[160,256]{1,0:T(8,128)}, f32[64,256]{1,0:T(8,128)}, f32[64,256]{1,0:T(8,128)}) custom-call(f32[160,256]{1,0:T(8,128)S(1)} %get-tuple-element.8.refs_0_, f32[160,256]{1,0:T(8,128)S(1)} %get-tuple-element.9.refs_1_, f32[64,256]{1,0:T(8,128)S(1)} %get-tuple-element.10.refs_2_, f32[64,256]{1,0:T(8,128)S(1)} %get-tuple-element.11.refs_3_), custom_call_target="tpu_custom_call" | custom-call | tf_op jit(solution)/shard_map/hand_over/pallas_call | solution.py:435
